TPU v7x, 256 devices: a whole 4x4x8 slice. The times are simulated.
256 devices in a mesh: frame: 16 (over x, y), expert: 16 (over z, core).
Axes of the slice: x: 4, y: 4, z: 8, core: 2. Of those that a mesh axis runs over, the one named last changes fastest.
Arguments:
- upstream: bfloat16 [16, 2048, 2048], P('frame', 'expert'), may hold values from -6 to 6
- saved: bfloat16 [16, 2048, 2048], P('frame', 'expert'), may hold values from -6 to 6
- expert_ids: int32 [16, 2048, 2], P('frame', 'expert'), may hold values from 0 to 15, all different within a row; in each aligned block of 128 rows (0 to 127, 128 to 255, ..., all dimensions but the last counted through in order) at most 32 rows name the same one
- gates: float32 [16, 2048, 2], P('frame', 'expert'), may hold values from 0.1 to 0.9
- weight_in: bfloat16 [16, 2048, 1024], P('expert'), may hold values from -0.125 to 0.125
- weight_out: bfloat16 [16, 2048, 1024], P('expert'), may hold values from -0.1875 to 0.1875
- spatial_rate: bfloat16 [16, 2048, 2048], P('frame', 'expert'), may hold values from 0 to 1
- temporal_rate: float32 [16, 2048], replicated, may hold values from 0 to 4.5
- scan_order: int32 [2048], P('expert'), may hold values from 0 to 2047, as said below
Outputs:
- result: bfloat16 [16, 2048, 2048], P('frame', 'expert')
- grad_in: bfloat16 [16, 2048, 1024], P('expert', 'frame')
- grad_out: bfloat16 [16, 2048, 1024], P('expert', 'frame')
Inputs may be any that keep to these rules, and one draw needn't show every extreme that they name: `expert_ids`: each row names 2 different experts. Among the 128 rows of one device, no expert is named by more than 32 rows, and in some devices one expert is named by exactly 32. `scan_order`: each aligned block of 128 scan steps visits exactly the tokens of the same block, in some order.
All inputs are finite; a program needn't handle non-finite values.
Results may differ from a plain program's by a relative error of at most 0.006.
Values may be sent and summed in bfloat16 or wider, within the bound.
No kernel may reach another device: no remote copies, remote signals or barrier semaphores. Data moves between devices by JAX's collectives and lax.ppermute only.
A program may use at most 192 MiB of HBM per device.

v0:
```python
import functools
import math

import jax
import jax.numpy as jnp
from jax import lax
from jax.experimental import pallas as pl
from jax.experimental.pallas import tpu as pltpu
from jax.sharding import PartitionSpec as P

TOPK = 2
LANES = 128
SUB = 8
VMEM_LIMIT = 20 * 1024 * 1024

GELU_SCALE = 0.7978845608028654
GELU_CUBIC = 0.044715


def gelu_parts(pre):
    inner = GELU_SCALE * (pre + GELU_CUBIC * pre * pre * pre)
    tangent = jnp.tanh(inner)
    value = 0.5 * pre * (1.0 + tangent)
    slope = 0.5 * (1.0 + tangent) + 0.5 * pre * (1.0 - tangent * tangent) * GELU_SCALE * (
        1.0 + 3.0 * GELU_CUBIC * pre * pre
    )
    return (value, slope)


def column_product(left, right):
    return lax.dot_general(
        left, right, (((0,), (0,)), ((), ())), preferred_element_type=jnp.float32
    )


def iota(shape, dim):
    return lax.broadcasted_iota(jnp.int32, shape, dim)


def call(kernel, out_shape, name, **kw):
    return pl.pallas_call(
        kernel,
        out_shape=out_shape,
        name=name,
        compiler_params=pltpu.CompilerParams(vmem_limit_bytes=VMEM_LIMIT),
        **kw,
    )


def facts_kernel(saved, ids_row, gates_row, out, marks, sems):
    rows, width = saved.shape
    body_copy = pltpu.make_async_copy(saved, out.at[:, 0:width], sems.at[0])
    body_copy.start()
    facts = [ids_row[k : k + 1, :].astype(jnp.float32) for k in range(TOPK)]
    for k in range(TOPK):
        rest = gates_row[k : k + 1, :]
        for _ in range(3):
            part = rest.astype(jnp.bfloat16).astype(jnp.float32)
            facts.append(part)
            rest = rest - part
    facts = jnp.concatenate(facts + [jnp.zeros((8, rows), jnp.float32)], axis=0)
    marks[...] = jnp.zeros((rows, LANES), jnp.bfloat16)
    marks[0:16, :] = facts.astype(jnp.bfloat16)
    marks_copy = pltpu.make_async_copy(marks, out.at[:, width : width + LANES], sems.at[1])
    marks_copy.start()
    marks_copy.wait()
    body_copy.wait()


def chosen_rows(facts, experts, x, width, gated, put):
    rows = x.shape[0]
    slots = 32 * len(experts)
    facts = facts[...].astype(jnp.float32)
    expert_of = jnp.concatenate([jnp.full((32, rows), e, jnp.int32) for e in experts], axis=0)
    expert_of = expert_of.astype(jnp.float32)
    slot_of = (iota((slots, rows), 0) % 32).astype(jnp.float32)
    first = facts[0:1] == expert_of
    hit = first | (facts[1:2] == expert_of)
    before = (iota((rows, rows), 0) < iota((rows, rows), 1)).astype(jnp.float32)
    rank = jnp.dot(
        hit.astype(jnp.float32).astype(jnp.bfloat16),
        before.astype(jnp.bfloat16),
        preferred_element_type=jnp.float32,
    )
    chosen = hit & (rank == slot_of)
    pick = chosen.astype(jnp.float32).astype(jnp.bfloat16)
    if gated:
        gate = jnp.where(
            first, facts[2:3] + facts[3:4] + facts[4:5], facts[5:6] + facts[6:7] + facts[7:8]
        )
        gate = jnp.sum(jnp.where(chosen, gate, 0.0), axis=1, keepdims=True)
    step = 512
    for c in range(0, width, step):
        part = jnp.dot(pick, x[:, c : c + step], preferred_element_type=jnp.float32)
        if gated:
            part = gate * part
        put(c, step, part.astype(jnp.bfloat16))


def pack_kernel(gated, me, facts_up, facts_down, up, down, pack_up, pack_down):
    z = me[0] // 2
    at = lambda n: (n + 16) % 16

    def put_in(out):
        def put(c, step, part):
            out[:, c : c + step] = part

        return put

    width = pack_up.shape[1]
    ahead = [at(2 * z + 2), at(2 * z + 3), at(2 * z + 4)]
    back = [at(2 * z - 2), at(2 * z - 1), at(2 * z - 3)]
    chosen_rows(facts_up, ahead, up, width, gated, put_in(pack_up))
    chosen_rows(facts_down, back, down, width, gated, put_in(pack_down))


NEAR = (0, -1, -2, 1, 2)
FAR = (-3, 3, 4)


def collect_kernel(gated, me, *refs):
    facts, sources = refs[:5], refs[5:10]
    up3, down3, up4, down4, own, other = refs[10:]
    e = me[0]
    core = e % 2
    for i in range(len(NEAR)):

        def put(c, step, part):
            own[32 * i : 32 * i + 32, c : c + step] = part[0:32]
            other[32 * i : 32 * i + 32, c : c + step] = part[32:64]

        experts = [e, e + 1 - 2 * core]
        chosen_rows(facts[i], experts, sources[i], own.shape[1], gated, put)
    mine = pl.ds(pl.multiple_of(core * 32, 32), 32)
    theirs = pl.ds(pl.multiple_of(32 - core * 32, 32), 32)
    own[160:192, :] = up3[mine, :]
    other[160:192, :] = up3[theirs, :]
    own[192:224, :] = down3[mine, :]
    other[192:224, :] = down3[theirs, :]

    @pl.when(core == 0)
    def _():
        own[224:256, :] = up4[...]
        other[224:256, :] = down4[...]

    @pl.when(core == 1)
    def _():
        own[224:256, :] = down4[...]
        other[224:256, :] = up4[...]


def forward_kernel(own, got, weight_in, inputs, hidden, slope, rows, sem):
    half = own.shape[0]
    rows[0:half, :] = own[...]
    rows[half : 2 * half, :] = got[...]
    copy = pltpu.make_async_copy(rows, inputs, sem)
    copy.start()
    step = 256
    for n in range(hidden.shape[1] // step):
        at = slice(n * step, (n + 1) * step)
        pre = jnp.dot(rows[...], weight_in[:, at], preferred_element_type=jnp.float32)
        value, rise = gelu_parts(pre)
        hidden[:, at] = value.astype(jnp.bfloat16)
        slope[:, at] = rise
    copy.wait()


def backward_kernel(
    me, own, got, weight_out, weight_in, slope, routed, back_pre, back, rows, pre, slots, sems
):
    half = own.shape[0]
    rows[0:half, :] = own[...]
    rows[half : 2 * half, :] = got[...]
    copies = [pltpu.make_async_copy(rows, routed, sems.at[0])]
    copies[0].start()
    step = 256
    for n in range(pre.shape[1] // step):
        at = slice(n * step, (n + 1) * step)
        back_hidden = jnp.dot(rows[...], weight_out[:, at], preferred_element_type=jnp.float32)
        pre[:, at] = (back_hidden * slope[:, at]).astype(jnp.bfloat16)
    copies.append(pltpu.make_async_copy(pre, back_pre, sems.at[1]))
    copies[1].start()
    e = me[0]
    z, core = e // 2, e % 2
    targets = []
    for owner in (core, 1 - core):
        targets += [2 * ((z + away + 8) % 8) + owner for away in NEAR + FAR]
    for n in range(weight_in.shape[0] // step):
        at = slice(n * step, (n + 1) * step)
        part = lax.dot_general(
            pre[...],
            weight_in[at, :],
            (((1,), (1,)), ((), ())),
            preferred_element_type=jnp.float32,
        ).astype(jnp.bfloat16)
        for i, target in enumerate(targets):
            slots[target, :, at] = part[32 * i : 32 * i + 32]
        copy = pltpu.make_async_copy(slots.at[:, :, at], back.at[:, :, at], sems.at[2 + n])
        copy.start()
        copies.append(copy)
    for copy in copies:
        copy.wait()


def grads_kernel(scale, along_y, place, left, right, *outs):
    x, y = place[0], place[1]
    for d in range(4):
        if along_y:
            frames = [4 * k + (y + d) % 4 for k in range(4)]
            lhs = [left[:, pl.ds(pl.multiple_of(f * LANES, LANES), LANES)] for f in frames]
            lhs = jnp.concatenate(lhs, axis=1)
        else:
            lhs = left[:, pl.ds(pl.multiple_of((x + d) % 4 * 512, 512), 512)]
        outs[d][...] = (column_product(lhs, right[...]) * scale).astype(jnp.bfloat16)


def sum_kernel(coordinate, place, p0, p1, p2, p3, *outs):
    at = place[coordinate]
    for d in range(4):
        rows = pl.ds(pl.multiple_of((at + d) % 4 * LANES, LANES), LANES)
        parts = [p[rows, :].astype(jnp.float32) for p in (p0, p1, p2, p3)]
        outs[d][...] = ((parts[0] + parts[1]) + (parts[2] + parts[3])).astype(outs[d].dtype)


def order_kernel(ids_col, order_col, upstream, undo, ordered):
    rows, slots = undo.shape
    expert_of = iota((rows, slots), 1) // 32
    slot_of = iota((rows, slots), 1) % 32
    hit = (ids_col[:, 0:1] == expert_of) | (ids_col[:, 1:2] == expert_of)
    before = (iota((rows, rows), 1) < iota((rows, rows), 0)).astype(jnp.bfloat16)
    rank = jnp.dot(
        before, hit.astype(jnp.float32).astype(jnp.bfloat16), preferred_element_type=jnp.float32
    )
    chosen = (hit & (rank.astype(jnp.int32) == slot_of)).astype(jnp.float32).astype(jnp.bfloat16)
    visit = (order_col[...] == iota((rows, rows), 1)).astype(jnp.float32).astype(jnp.bfloat16)
    undo[...] = jnp.dot(visit, chosen, preferred_element_type=jnp.float32).astype(jnp.bfloat16)
    ordered[...] = jnp.dot(visit, upstream[...], preferred_element_type=jnp.float32).astype(
        jnp.bfloat16
    )


def tile_decays(rate8, beyond):
    row = iota(rate8.shape, 0)
    shifted = pltpu.roll(rate8, SUB - 1, 0)
    e1 = jnp.where(row < 7, shifted, beyond)
    e2 = e1 + pltpu.roll(e1, SUB - 1, 0)
    e4 = e2 + pltpu.roll(e2, SUB - 2, 0)
    s1 = jnp.where(row < 7, e2, e1)
    s2 = s1 + jnp.where(row < 6, pltpu.roll(s1, SUB - 2, 0), 0.0)
    s4 = s2 + jnp.where(row < 4, pltpu.roll(s2, SUB - 4, 0), 0.0)
    return row, e1, e2, e4, s4, shifted


def undo_kernel(undo, returned, after, mixed):
    blocks = mixed.shape[0]
    pick = undo[...]
    step = 512
    for c in range(0, blocks * LANES, step):
        part = jnp.dot(pick, returned[:, c : c + step], preferred_element_type=jnp.float32).astype(
            jnp.bfloat16
        )
        for b in range(step // LANES):
            mixed[c // LANES + b] = part[:, b * LANES : (b + 1) * LANES]


def temporal_kernel(pencil, keep, inject, *refs):
    out = refs[-1]
    frames = pencil.shape[0]
    carry = jnp.zeros(pencil.shape[1:], jnp.float32)
    for f in reversed(range(frames)):
        total = pencil[f].astype(jnp.float32) + carry
        out[f] = (inject[f : f + 1, :] * total).astype(jnp.bfloat16)
        carry = keep[f : f + 1, :] * total


def scan_kernel(spatial, rate, *refs):
    local, send, head = refs[-3:]
    blocks, rows, _ = spatial.shape
    group = 4
    wide = group * LANES
    for q in range(blocks // group):
        at = slice(q * wide, (q + 1) * wide)
        carry = jnp.zeros((1, wide), jnp.float32)
        later = jnp.zeros((1, wide), jnp.float32)
        beyond = jnp.zeros((SUB, wide), jnp.float32)
        for pair in reversed(range(rows // 16)):
            two = slice(pair * 16, pair * 16 + 16)
            rates = rate[two, at].astype(jnp.float32)
            values = [spatial[q * group + k, two, :].astype(jnp.float32) for k in range(group)]
            values = jnp.concatenate(values, axis=1)
            for half in (1, 0):
                part = slice(half * SUB, half * SUB + SUB)
                row, e1, e2, e4, s4, beyond = tile_decays(rates[part], beyond)
                value = values[part]
                near = jnp.where(row < 7, jnp.exp(-e1), 0.0)
                value = value + near * pltpu.roll(value, SUB - 1, 0)
                near = jnp.where(row < 6, jnp.exp(-e2), 0.0)
                value = value + near * pltpu.roll(value, SUB - 2, 0)
                near = jnp.where(row < 4, jnp.exp(-e4), 0.0)
                value = value + near * pltpu.roll(value, SUB - 4, 0)
                value = value + jnp.exp(-s4) * carry
                local[pair * 16 + half * SUB : pair * 16 + half * SUB + SUB, at] = value
                carry = value[0:1]
                later = later + s4[0:1]
        start = rate[0:16, at].astype(jnp.float32)[0:1]
        top = jnp.exp(-start) * carry
        keep = jnp.exp(-(later + start))
        for k in range(group):
            b = q * group + k
            head[b : b + 1, :] = top[:, k * LANES : (k + 1) * LANES]
            head[blocks + b : blocks + b + 1, :] = keep[:, k * LANES : (k + 1) * LANES]
    everyone = head[...]
    for e in range(send.shape[0]):
        send[e] = everyone


def combine_kernel(rate, inject, local, ordered, base, reach):
    rows, width = local.shape
    wide = 4 * LANES
    for q in range(width // wide):
        at = slice(q * wide, (q + 1) * wide)
        later = jnp.zeros((1, wide), jnp.float32)
        beyond = jnp.zeros((SUB, wide), jnp.float32)
        for pair in reversed(range(rows // 16)):
            two = slice(pair * 16, pair * 16 + 16)
            rates = rate[two, at].astype(jnp.float32)
            strong = inject[two, at]
            base[two, at] = ordered[two, at].astype(jnp.float32) + strong * local[two, at]
            for half in (1, 0):
                part = slice(half * SUB, half * SUB + SUB)
                _, _, _, _, s4, beyond = tile_decays(rates[part], beyond)
                here = slice(pair * 16 + half * SUB, pair * 16 + half * SUB + SUB)
                reach[here, at] = strong[part] * jnp.exp(-(s4 + later))
                later = later + s4[0:1]


def finish_kernel(me, order_row, heads, base, reach, out, scratch):
    rows, width = base.shape
    experts, doubled, _ = heads.shape
    blocks = doubled // 2
    carry = jnp.zeros((blocks, LANES), jnp.float32)
    for e in reversed(range(1, experts)):
        through = heads[e, 0:blocks, :] + heads[e, blocks:doubled, :] * carry
        carry = jnp.where(e > me[0], through, carry)
    scratch[...] = carry
    back = (order_row[...] == iota((rows, rows), 0)).astype(jnp.float32).astype(jnp.bfloat16)
    first = pl.program_id(0) * (width // LANES)
    for b in range(width // LANES):
        at = slice(b * LANES, (b + 1) * LANES)
        value = base[:, at] + reach[:, at] * scratch[pl.ds(first + b, 1), :]
        out[:, at] = jnp.dot(
            back, value.astype(jnp.bfloat16), preferred_element_type=jnp.float32
        ).astype(jnp.bfloat16)


def body(
    upstream,
    saved,
    expert_ids,
    gates,
    weight_in,
    weight_out,
    spatial_rate,
    temporal_rate,
    scan_order,
):
    experts = lax.axis_size("expert")
    frames = lax.axis_size("frame")
    rows = upstream.shape[1]
    width = upstream.shape[2]
    hidden_width = weight_in.shape[2]
    capacity = 2 * TOPK * rows // experts
    slots = experts * capacity
    blocks = width // LANES
    f32, bf16 = jnp.float32, jnp.bfloat16
    shape = jax.ShapeDtypeStruct
    me = lax.axis_index("expert")

    up = [(i, (i + 2) % experts) for i in range(experts)]
    down = [(i, (i - 2) % experts) for i in range(experts)]
    swap = [(i, i ^ 1) for i in range(experts)]
    scalar = me.astype(jnp.int32).reshape(1)
    smem = pl.BlockSpec(memory_space=pltpu.SMEM)
    vmem = pl.BlockSpec(memory_space=pltpu.VMEM)

    ids_col = expert_ids[0]
    rate = spatial_rate[0]
    tail = pl.BlockSpec((16, LANES), lambda i: (0, blocks))
    whole = lambda shape: pl.BlockSpec(shape, lambda i: (0, 0))
    far = pl.BlockSpec(memory_space=pltpu.HBM)
    marked = call(
        facts_kernel,
        pltpu.HBM((rows, width + LANES), bf16),
        "facts",
        in_specs=[far, vmem, vmem],
        out_specs=far,
        scratch_shapes=[pltpu.VMEM((rows, LANES), bf16), pltpu.SemaphoreType.DMA((2,))],
    )(saved[0], ids_col.T, gates[0].T)
    chains = []
    for x in (marked, upstream[0]):
        up1, down1 = lax.ppermute(x, "expert", up), lax.ppermute(x, "expert", down)
        chains.append([x, up1, lax.ppermute(up1, "expert", up), down1])
        chains[-1].append(lax.ppermute(down1, "expert", down))
    facts = chains[0]
    pieces = []
    for gated, chain in enumerate(chains):
        full = whole(chain[0].shape)
        packed = call(
            functools.partial(pack_kernel, bool(gated)),
            (shape((96, width), bf16),) * 2,
            "pack",
            grid=(1,),
            in_specs=[smem] + [tail] * 2 + [full] * 2,
            out_specs=[whole((96, width))] * 2,
        )(scalar, facts[2], facts[4], chain[2], chain[4])
        up3 = lax.ppermute(packed[0], "expert", up)
        down3 = lax.ppermute(packed[1], "expert", down)
        up4 = lax.ppermute(up3[64:96], "expert", up)
        down4 = lax.ppermute(down3[64:96], "expert", down)
        ends = [whole((96, width))] * 2 + [whole((32, width))] * 2
        own, other = call(
            functools.partial(collect_kernel, bool(gated)),
            (shape((256, width), bf16),) * 2,
            "collect",
            grid=(1,),
            in_specs=[smem] + [tail] * 5 + [full] * 5 + ends,
            out_specs=[whole((256, width))] * 2,
        )(scalar, *facts, *chain, up3, down3, up4, down4)
        pieces.append((own, lax.ppermute(other, "expert", swap)))

    local_order = scan_order - me * rows
    undo, ordered = call(
        order_kernel, (shape((rows, slots), bf16), shape((rows, width), bf16)), "order"
    )(ids_col, local_order.reshape(rows, 1), upstream[0])
    inject = jnp.sqrt(-jnp.expm1(-2.0 * rate.astype(f32)))
    own_rate = lax.dynamic_slice_in_dim(
        temporal_rate, lax.axis_index("frame") * (width // frames), width // frames, axis=1
    )
    keep_time = jnp.exp(-own_rate)
    inject_time = jnp.sqrt(-jnp.expm1(-2.0 * own_rate))

    weight_in_one = weight_in[0]
    weight_out_one = weight_out[0]
    scale = 1.0 / math.sqrt(rows * experts * frames * upstream.shape[0])
    dma = pltpu.SemaphoreType.DMA
    inputs_all, hidden, slope = call(
        forward_kernel,
        (
            pltpu.HBM((slots, width), bf16),
            shape((slots, hidden_width), bf16),
            shape((slots, hidden_width), f32),
        ),
        "forward",
        out_specs=(far, vmem, vmem),
        scratch_shapes=[pltpu.VMEM((slots, width), bf16), dma(())],
    )(*pieces[0], weight_in_one)
    routed_all, back_pre, back_slots = call(
        backward_kernel,
        (
            pltpu.HBM((slots, width), bf16),
            pltpu.HBM((slots, hidden_width), bf16),
            pltpu.HBM((experts, capacity, width), bf16),
        ),
        "backward",
        in_specs=[smem] + [vmem] * 5,
        out_specs=(far, far, far),
        scratch_shapes=[
            pltpu.VMEM((slots, width), bf16),
            pltpu.VMEM((slots, hidden_width), bf16),
            pltpu.VMEM((experts, capacity, width), bf16),
            dma((2 + width // 256,)),
        ],
    )(scalar, *pieces[1], weight_out_one, weight_in_one, slope)
    returned = lax.all_to_all(
        back_slots, "expert", split_axis=0, concat_axis=0, tiled=True
    ).reshape(slots, width)
    frame = lax.axis_index("frame")
    place = jnp.stack([frame // 4, frame % 4]).astype(jnp.int32)
    along_x = [[(i, (i // 4 + d) % 4 * 4 + i % 4) for i in range(frames)] for d in range(4)]
    along_y = [[(i, i // 4 * 4 + (i % 4 + d) % 4) for i in range(frames)] for d in range(4)]
    grads, sums, moves = [], [], []
    for name, left, right, axes, turn in (
        ("grads_out", routed_all, hidden, (along_x, along_y), 1),
        ("grads_in", inputs_all, back_pre, (along_y, along_x), 0),
    ):
        quarter = (width // 4, hidden_width)
        parts = call(
            functools.partial(grads_kernel, scale, turn == 0),
            (pltpu.HBM(quarter, bf16),) * 4,
            name,
            in_specs=[smem] + [vmem] * 2,
        )(place, left, right)
        parts = [parts[0]] + [lax.ppermute(parts[d], "frame", axes[0][d]) for d in (1, 3, 2)]
        parts = call(
            functools.partial(sum_kernel, turn),
            tuple(pltpu.HBM((LANES, hidden_width), bf16 if d else f32) for d in range(4)),
            "sum_" + name,
            in_specs=[smem] + [vmem] * 4,
        )(place, *parts)
        moved = [lax.ppermute(parts[d], "frame", axes[1][d]) for d in (1, 3, 2)]
        sums.append(parts[0])
        moves.append(moved)
        total = parts[0] + moved[0].astype(f32) + moved[1].astype(f32) + moved[2].astype(f32)
        grads.append(total.astype(bf16)[None])
    grad_out, grad_in = grads

    mixed = call(
        undo_kernel,
        shape((blocks, rows, LANES), bf16),
        "undo",
        in_specs=[vmem, vmem, far],
    )(undo, returned, sums[0])
    pencil = lax.all_to_all(mixed, "frame", split_axis=0, concat_axis=0, tiled=True)
    pencil = call(
        temporal_kernel,
        shape(pencil.shape, bf16),
        "temporal",
        in_specs=[vmem] * 3 + [far] * 4,
    )(pencil, keep_time, inject_time, sums[1], *moves[0])
    spatial = lax.all_to_all(pencil, "frame", split_axis=0, concat_axis=0, tiled=True)
    local, heads = call(
        scan_kernel,
        (shape((rows, width), f32), shape((experts, 2 * blocks, LANES), f32)),
        "scan",
        in_specs=[vmem] * 2 + [far] * 3,
        scratch_shapes=[pltpu.VMEM((2 * blocks, LANES), f32)],
    )(spatial, rate, *moves[1])
    heads = lax.all_to_all(heads, "expert", split_axis=0, concat_axis=0, tiled=True)
    base, reach = call(combine_kernel, (pltpu.HBM((rows, width), f32),) * 2, "combine")(
        rate, inject, local, ordered
    )
    chunk = pl.BlockSpec((rows, 4 * LANES), lambda i: (0, i))
    result = call(
        finish_kernel,
        shape((rows, width), bf16),
        "finish",
        grid=(blocks // 4,),
        in_specs=[
            smem,
            whole((1, rows)),
            pl.BlockSpec(heads.shape, lambda i: (0, 0, 0)),
            chunk,
            chunk,
        ],
        out_specs=chunk,
        scratch_shapes=[pltpu.VMEM((blocks, LANES), f32)],
    )(scalar, local_order.reshape(1, rows), heads, base, reach)
    return (result[None], grad_in, grad_out)


def solution(mesh):
    in_specs = (
        P("frame", "expert", None),
        P("frame", "expert", None),
        P("frame", "expert", None),
        P("frame", "expert", None),
        P("expert", None, None),
        P("expert", None, None),
        P("frame", "expert", None),
        P(),
        P("expert"),
    )
    out_specs = (P("frame", "expert", None), P("expert", "frame", None), P("expert", "frame", None))
    return jax.shard_map(body, mesh=mesh, in_specs=in_specs, out_specs=out_specs, check_vma=False)
```

profile of v0, /device:TPU:1, one launch (start us, length us, event | category | flops | bytes accessed | tf_op | source)
XLA Modules:
  0.0 259.3 jit_solution(11082079747859061976)
XLA Ops:
  6.4 4.0 %collective-permute-start.2 = (bf16[128,2176]{1,0:T(8,128)(2,1)}, bf16[128,2176]{1,0:T(8,128)(2,1)S(1)}, u32[]{:S(2)}, u32[]{:S(2)}) collective-permute-start(bf16[128,2176]{1,0:T(8,128)(2,1)} %facts.1.refs_0_.refs_5_), channel_id=1, source_target_pairs={{0,14},{1,15},{2,0},{3,1},{4,2},{5,3},{6,4},{7,5},{8,6},{9,7},{10,... | collective-permute-start | bytes 1671176 | tf_op jit(solution)/shard_map/ppermute | solution.py:401
  13.1 9.8 %collective-permute-done.refs_1_.refs_6_ = bf16[128,2176]{1,0:T(8,128)(2,1)S(1)} collective-permute-done((bf16[128,2176]{1,0:T(8,128)(2,1)}, bf16[128,2176]{1,0:T(8,128)(2,1)S(1)}, u32[]{:S(2)}, u32[]{:S(2)}) %collective-permute-start) | collective-permute-done | bytes 557088 | tf_op jit(solution)/shard_map/ppermute | solution.py:401
  25.6 8.7 %collective-permute-done.4.refs_6_ = bf16[128,2048]{1,0:T(8,128)(2,1)} collective-permute-done((bf16[128,2048]{1,0:T(8,128)(2,1)}, bf16[128,2048]{1,0:T(8,128)(2,1)}, u32[]{:S(2)}, u32[]{:S(2)}) %collective-permute-start.4) | collective-permute-done | bytes 524320 | tf_op jit(solution)/shard_map/ppermute | solution.py:401
  37.0 9.2 %collective-permute-done.1.facts_up.refs_2_.up.refs_7_ = bf16[128,2176]{1,0:T(8,128)(2,1)S(1)} collective-permute-done((bf16[128,2176]{1,0:T(8,128)(2,1)S(1)}, bf16[128,2176]{1,0:T(8,128)(2,1)S(1)}, u32[]{:S(2)}, u32[]{:S(2)}) %collective-permute-start.1) | collective-permute-done | bytes 557088 | tf_op jit(solution)/shard_map/ppermute | solution.py:402
  49.5 7.8 %collective-permute-done.5.up.refs_7_ = bf16[128,2048]{1,0:T(8,128)(2,1)S(1)} collective-permute-done((bf16[128,2048]{1,0:T(8,128)(2,1)}, bf16[128,2048]{1,0:T(8,128)(2,1)S(1)}, u32[]{:S(2)}, u32[]{:S(2)}) %collective-permute-start.5) | collective-permute-done | bytes 524320 | tf_op jit(solution)/shard_map/ppermute | solution.py:402
  60.7 5.0 %collective-permute-done.13.refs_10_ = bf16[96,2048]{1,0:T(8,128)(2,1)S(1)} collective-permute-done((bf16[96,2048]{1,0:T(8,128)(2,1)S(1)}, bf16[96,2048]{1,0:T(8,128)(2,1)S(1)}, u32[]{:S(2)}, u32[]{:S(2)}) %collective-permute-start.13) | collective-permute-done | bytes 393248 | tf_op jit(solution)/shard_map/ppermute | solution.py:416
  68.6 5.6 %collective-permute-done.8.refs_10_ = bf16[96,2048]{1,0:T(8,128)(2,1)S(1)} collective-permute-done((bf16[96,2048]{1,0:T(8,128)(2,1)S(1)}, bf16[96,2048]{1,0:T(8,128)(2,1)S(1)}, u32[]{:S(2)}, u32[]{:S(2)}) %collective-permute-start.8) | collective-permute-done | bytes 393248 | tf_op jit(solution)/shard_map/ppermute | solution.py:416
  85.3 3.5 %forward.1 = (bf16[512,2048]{1,0:T(8,128)(2,1)}, bf16[512,1024]{1,0:T(8,128)(2,1)S(1)}, f32[512,1024]{1,0:T(8,128)S(1)}) custom-call(bf16[256,2048]{1,0:T(8,128)(2,1)S(1)} %get-tuple-element.46.own, bf16[256,2048]{1,0:T(8,128)(2,1)S(1)} %collective-permute-done.17.got, bf16[2048,1024]{1,0:T(8,128)(2,1)S(1)} %bitcast.25), custom_call_target="tpu_custom_call" | custom-call | tf_op jit(solution)/shard_map/forward/pallas_call | solution.py:446
  88.8 5.6 %backward.1 = (bf16[512,2048]{1,0:T(8,128)(2,1)}, bf16[512,1024]{1,0:T(8,128)(2,1)}, bf16[16,32,2048]{2,1,0:T(8,128)(2,1)}) custom-call(s32[1]{0:T(128)} %bitcast.me, bf16[256,2048]{1,0:T(8,128)(2,1)S(1)} %get-tuple-element.42.own, bf16[256,2048]{1,0:T(8,128)(2,1)S(1)} %collective-permute-done.12.got, bf16[2048,1024]{1,0:T(8,128)(2,1)S(1)} %bitcast.30, ...), custom_call_target="tpu_custom_call" | custom-call | tf_op jit(solution)/shard_map/backward/pallas_call | solution.py:457
  94.4 6.7 %all-to-all-start = ((bf16[16,32,2048]{2,1,0:T(8,128)(2,1)}), bf16[16,32,2048]{2,1,0:T(8,128)(2,1)S(1)}, u32[]{:S(2)}, u32[]{:S(2)}) async-start(bf16[16,32,2048]{2,1,0:T(8,128)(2,1)} %get-tuple-element.49), calls=%async_computation | async-start | bytes 4194304 | tf_op jit(solution)/shard_map/all_to_all | solution.py:474
  104.1 4.3 %grads_out.1 = (bf16[512,1024]{1,0:T(8,128)(2,1)}, bf16[512,1024]{1,0:T(8,128)(2,1)}, bf16[512,1024]{1,0:T(8,128)(2,1)}, bf16[512,1024]{1,0:T(8,128)(2,1)}) custom-call(s32[2]{0:T(128)S(1)} %pad_add_fusion.place, bf16[512,2048]{1,0:T(8,128)(2,1)S(1)} %copy-done.10, bf16[512,1024]{1,0:T(8,128)(2,1)S(1)} %copy-done.21), custom_call_target="tpu_custom_call" | custom-call | tf_op jit(solution)/shard_map/grads_out/pallas_call | solution.py:487
  108.4 9.8 %collective-permute-start.18 = (bf16[512,1024]{1,0:T(8,128)(2,1)}, bf16[512,1024]{1,0:T(8,128)(2,1)S(1)}, u32[]{:S(2)}, u32[]{:S(2)}) collective-permute-start(bf16[512,1024]{1,0:T(8,128)(2,1)} %get-tuple-element.53), channel_id=1, source_target_pairs={{0,64},{16,80},{32,96},{48,112},{64,128},{80,144},{96,160},{112,17... | collective-permute-start | bytes 3145736 | tf_op jit(solution)/shard_map/ppermute | solution.py:493
  121.2 4.3 %grads_in.1 = (bf16[512,1024]{1,0:T(8,128)(2,1)}, bf16[512,1024]{1,0:T(8,128)(2,1)}, bf16[512,1024]{1,0:T(8,128)(2,1)}, bf16[512,1024]{1,0:T(8,128)(2,1)}) custom-call(s32[2]{0:T(128)S(1)} %pad_add_fusion.place, bf16[512,2048]{1,0:T(8,128)(2,1)S(1)} %copy-done.9, bf16[512,1024]{1,0:T(8,128)(2,1)S(1)} %copy-done.19), custom_call_target="tpu_custom_call" | custom-call | tf_op jit(solution)/shard_map/grads_in/pallas_call | solution.py:487
  128.2 14.9 %collective-permute-done.18.p1 = bf16[512,1024]{1,0:T(8,128)(2,1)S(1)} collective-permute-done((bf16[512,1024]{1,0:T(8,128)(2,1)}, bf16[512,1024]{1,0:T(8,128)(2,1)S(1)}, u32[]{:S(2)}, u32[]{:S(2)}) %collective-permute-start.18) | collective-permute-done | bytes 1048608 | tf_op jit(solution)/shard_map/ppermute | solution.py:493
  148.6 18.0 %collective-permute-done.20.p3 = bf16[512,1024]{1,0:T(8,128)(2,1)} collective-permute-done((bf16[512,1024]{1,0:T(8,128)(2,1)}, bf16[512,1024]{1,0:T(8,128)(2,1)}, u32[]{:S(2)}, u32[]{:S(2)}) %collective-permute-start.20) | collective-permute-done | bytes 1048608 | tf_op jit(solution)/shard_map/ppermute | solution.py:493
  174.3 5.1 %all-to-all-start.1 = ((bf16[16,128,128]{2,1,0:T(8,128)(2,1)}), bf16[16,128,128]{2,1,0:T(8,128)(2,1)S(1)}, u32[]{:S(2)}, u32[]{:S(2)}) async-start(bf16[16,128,128]{2,1,0:T(8,128)(2,1)} %undo.1), calls=%async_computation.1 | async-start | bytes 1048576 | tf_op jit(solution)/shard_map/all_to_all | solution.py:513
  184.5 3.3 %sum_grads_in.1 = (f32[128,1024]{1,0:T(8,128)}, bf16[128,1024]{1,0:T(8,128)(2,1)}, bf16[128,1024]{1,0:T(8,128)(2,1)}, bf16[128,1024]{1,0:T(8,128)(2,1)}) custom-call(s32[2]{0:T(128)S(1)} %pad_add_fusion.place, bf16[512,1024]{1,0:T(8,128)(2,1)S(1)} %copy-done.13, bf16[512,1024]{1,0:T(8,128)(2,1)} %collective-permute-done.21.p1, ...), custom_call_target="tpu_custom_call" | custom-call | tf_op jit(solution)/shard_map/sum_grads_in/pallas_call | solution.py:494
  187.8 5.1 %collective-permute-done.24.refs_1_ = bf16[128,1024]{1,0:T(8,128)(2,1)S(1)} collective-permute-done((bf16[128,1024]{1,0:T(8,128)(2,1)}, bf16[128,1024]{1,0:T(8,128)(2,1)S(1)}, u32[]{:S(2)}, u32[]{:S(2)}) %collective-permute-start.24) | collective-permute-done | bytes 262176 | tf_op jit(solution)/shard_map/ppermute | solution.py:500
  193.0 6.0 %collective-permute-done.26.refs_3_ = bf16[128,1024]{1,0:T(8,128)(2,1)S(1)} collective-permute-done((bf16[128,1024]{1,0:T(8,128)(2,1)}, bf16[128,1024]{1,0:T(8,128)(2,1)S(1)}, u32[]{:S(2)}, u32[]{:S(2)}) %collective-permute-start.26) | collective-permute-done | bytes 262176 | tf_op jit(solution)/shard_map/ppermute | solution.py:500
  201.1 5.5 %all-to-all-start.2 = ((bf16[16,128,128]{2,1,0:T(8,128)(2,1)}), bf16[16,128,128]{2,1,0:T(8,128)(2,1)S(1)}, u32[]{:S(2)}, u32[]{:S(2)}) async-start(bf16[16,128,128]{2,1,0:T(8,128)(2,1)} %temporal.1), calls=%async_computation.2 | async-start | bytes 1048576 | tf_op jit(solution)/shard_map/all_to_all | solution.py:520
  211.9 9.1 %collective-permute-done.27.refs_0_ = bf16[128,1024]{1,0:T(8,128)(2,1)S(1)} collective-permute-done((bf16[128,1024]{1,0:T(8,128)(2,1)}, bf16[128,1024]{1,0:T(8,128)(2,1)S(1)}, u32[]{:S(2)}, u32[]{:S(2)}) %collective-permute-start.27) | collective-permute-done | bytes 262176 | tf_op jit(solution)/shard_map/ppermute | solution.py:500
  222.4 3.4 %collective-permute-done.29.refs_2_ = bf16[128,1024]{1,0:T(8,128)(2,1)S(1)} collective-permute-done((bf16[128,1024]{1,0:T(8,128)(2,1)}, bf16[128,1024]{1,0:T(8,128)(2,1)S(1)}, u32[]{:S(2)}, u32[]{:S(2)}) %collective-permute-start.29) | collective-permute-done | bytes 262176 | tf_op jit(solution)/shard_map/ppermute | solution.py:500
  232.6 9.2 %all-to-all-start.3 = ((f32[16,32,128]{2,1,0:T(8,128)}), f32[16,32,128]{2,1,0:T(8,128)}, u32[]{:S(2)}, u32[]{:S(2)}) async-start(f32[16,32,128]{2,1,0:T(8,128)} %copy-done.37), calls=%async_computation.3 | async-start | bytes 524288 | tf_op jit(solution)/shard_map/all_to_all | solution.py:528
  246.7 6.8 %all-to-all-done.3.heads = f32[16,32,128]{2,1,0:T(8,128)} async-done(((f32[16,32,128]{2,1,0:T(8,128)}), f32[16,32,128]{2,1,0:T(8,128)}, u32[]{:S(2)}, u32[]{:S(2)}) %all-to-all-start.3) | async-done | bytes 262176 | tf_op jit(solution)/shard_map/all_to_all | solution.py:528
  (157 shorter events, 87.4 us)
Async XLA Ops:
  3.9 19.0 %collective-permute-start = (bf16[128,2176]{1,0:T(8,128)(2,1)}, bf16[128,2176]{1,0:T(8,128)(2,1)S(1)}, u32[]{:S(2)}, u32[]{:S(2)}) collective-permute-start(bf16[128,2176]{1,0:T(8,128)(2,1)} %facts.1.refs_0_.refs_5_), channel_id=1, source_target_pairs={{0,2},{1,3},{2,4},{3,5},{4,6},{5,7},{6,8},{7,9},{8,10},{9,11},{10,... | collective-permute-start | bytes 1671176 | tf_op jit(solution)/shard_map/ppermute | solution.py:401
  6.4 16.5 %collective-permute-start.2 = (bf16[128,2176]{1,0:T(8,128)(2,1)}, bf16[128,2176]{1,0:T(8,128)(2,1)S(1)}, u32[]{:S(2)}, u32[]{:S(2)}) collective-permute-start(bf16[128,2176]{1,0:T(8,128)(2,1)} %facts.1.refs_0_.refs_5_), channel_id=1, source_target_pairs={{0,14},{1,15},{2,0},{3,1},{4,2},{5,3},{6,4},{7,5},{8,6},{9,7},{10,... | collective-permute-start | bytes 1671176 | tf_op jit(solution)/shard_map/ppermute | solution.py:401
  10.5 23.8 %collective-permute-start.4 = (bf16[128,2048]{1,0:T(8,128)(2,1)}, bf16[128,2048]{1,0:T(8,128)(2,1)}, u32[]{:S(2)}, u32[]{:S(2)}) collective-permute-start(bf16[128,2048]{1,0:T(8,128)(2,1)} %bitcast.31), channel_id=1, source_target_pairs={{0,2},{1,3},{2,4},{3,5},{4,6},{5,7},{6,8},{7,9},{8,10},{9,11},{10,... | collective-permute-start | bytes 1572872 | tf_op jit(solution)/shard_map/ppermute | solution.py:401
  10.5 23.8 %collective-permute-start.6 = (bf16[128,2048]{1,0:T(8,128)(2,1)}, bf16[128,2048]{1,0:T(8,128)(2,1)}, u32[]{:S(2)}, u32[]{:S(2)}) collective-permute-start(bf16[128,2048]{1,0:T(8,128)(2,1)} %bitcast.32), channel_id=1, source_target_pairs={{0,14},{1,15},{2,0},{3,1},{4,2},{5,3},{6,4},{7,5},{8,6},{9,7},{10,... | collective-permute-start | bytes 1572872 | tf_op jit(solution)/shard_map/ppermute | solution.py:401
  22.9 23.2 %collective-permute-start.1 = (bf16[128,2176]{1,0:T(8,128)(2,1)S(1)}, bf16[128,2176]{1,0:T(8,128)(2,1)S(1)}, u32[]{:S(2)}, u32[]{:S(2)}) collective-permute-start(bf16[128,2176]{1,0:T(8,128)(2,1)S(1)} %collective-permute-done.refs_1_.refs_6_), channel_id=1, source_target_pairs={{0,2},{1,3},{2,4},{3,5},{4,6},{5,7},{6,8},{7,9},{8,10},{9,11},{10,... | collective-permute-start | bytes 1671176 | tf_op jit(solution)/shard_map/ppermute | solution.py:402
  22.9 23.2 %collective-permute-start.3 = (bf16[128,2176]{1,0:T(8,128)(2,1)S(1)}, bf16[128,2176]{1,0:T(8,128)(2,1)S(1)}, u32[]{:S(2)}, u32[]{:S(2)}) collective-permute-start(bf16[128,2176]{1,0:T(8,128)(2,1)S(1)} %collective-permute-done.2.refs_3_.refs_8_), channel_id=1, source_target_pairs={{0,14},{1,15},{2,0},{3,1},{4,2},{5,3},{6,4},{7,5},{8,6},{9,7},{10,... | collective-permute-start | bytes 1671176 | tf_op jit(solution)/shard_map/ppermute | solution.py:403
  34.3 23.1 %collective-permute-start.5 = (bf16[128,2048]{1,0:T(8,128)(2,1)}, bf16[128,2048]{1,0:T(8,128)(2,1)S(1)}, u32[]{:S(2)}, u32[]{:S(2)}) collective-permute-start(bf16[128,2048]{1,0:T(8,128)(2,1)} %collective-permute-done.4.refs_6_), channel_id=1, source_target_pairs={{0,2},{1,3},{2,4},{3,5},{4,6},{5,7},{6,8},{7,9},{8,10},{9,11},{10,... | collective-permute-start | bytes 1572872 | tf_op jit(solution)/shard_map/ppermute | solution.py:402
  34.3 23.1 %collective-permute-start.7 = (bf16[128,2048]{1,0:T(8,128)(2,1)}, bf16[128,2048]{1,0:T(8,128)(2,1)S(1)}, u32[]{:S(2)}, u32[]{:S(2)}) collective-permute-start(bf16[128,2048]{1,0:T(8,128)(2,1)} %collective-permute-done.6.refs_8_), channel_id=1, source_target_pairs={{0,14},{1,15},{2,0},{3,1},{4,2},{5,3},{6,4},{7,5},{8,6},{9,7},{10,... | collective-permute-start | bytes 1572872 | tf_op jit(solution)/shard_map/ppermute | solution.py:403
  46.7 19.0 %collective-permute-start.13 = (bf16[96,2048]{1,0:T(8,128)(2,1)S(1)}, bf16[96,2048]{1,0:T(8,128)(2,1)S(1)}, u32[]{:S(2)}, u32[]{:S(2)}) collective-permute-start(bf16[96,2048]{1,0:T(8,128)(2,1)S(1)} %get-tuple-element.44), channel_id=1, source_target_pairs={{0,2},{1,3},{2,4},{3,5},{4,6},{5,7},{6,8},{7,9},{8,10},{9,11},{10,... | collective-permute-start | bytes 1179656 | tf_op jit(solution)/shard_map/ppermute | solution.py:416
  46.8 19.0 %collective-permute-start.14 = (bf16[96,2048]{1,0:T(8,128)(2,1)S(1)}, bf16[96,2048]{1,0:T(8,128)(2,1)S(1)}, u32[]{:S(2)}, u32[]{:S(2)}) collective-permute-start(bf16[96,2048]{1,0:T(8,128)(2,1)S(1)} %get-tuple-element.45), channel_id=1, source_target_pairs={{0,14},{1,15},{2,0},{3,1},{4,2},{5,3},{6,4},{7,5},{8,6},{9,7},{10,... | collective-permute-start | bytes 1179656 | tf_op jit(solution)/shard_map/ppermute | solution.py:417
  58.0 16.2 %collective-permute-start.8 = (bf16[96,2048]{1,0:T(8,128)(2,1)S(1)}, bf16[96,2048]{1,0:T(8,128)(2,1)S(1)}, u32[]{:S(2)}, u32[]{:S(2)}) collective-permute-start(bf16[96,2048]{1,0:T(8,128)(2,1)S(1)} %get-tuple-element.40), channel_id=1, source_target_pairs={{0,2},{1,3},{2,4},{3,5},{4,6},{5,7},{6,8},{7,9},{8,10},{9,11},{10,... | collective-permute-start | bytes 1179656 | tf_op jit(solution)/shard_map/ppermute | solution.py:416
  58.1 16.5 %collective-permute-start.9 = (bf16[96,2048]{1,0:T(8,128)(2,1)S(1)}, bf16[96,2048]{1,0:T(8,128)(2,1)S(1)}, u32[]{:S(2)}, u32[]{:S(2)}) collective-permute-start(bf16[96,2048]{1,0:T(8,128)(2,1)S(1)} %get-tuple-element.41), channel_id=1, source_target_pairs={{0,14},{1,15},{2,0},{3,1},{4,2},{5,3},{6,4},{7,5},{8,6},{9,7},{10,... | collective-permute-start | bytes 1179656 | tf_op jit(solution)/shard_map/ppermute | solution.py:417
  94.4 77.6 %all-to-all-start = ((bf16[16,32,2048]{2,1,0:T(8,128)(2,1)}), bf16[16,32,2048]{2,1,0:T(8,128)(2,1)S(1)}, u32[]{:S(2)}, u32[]{:S(2)}) async-start(bf16[16,32,2048]{2,1,0:T(8,128)(2,1)} %get-tuple-element.49), calls=%async_computation | async-start | bytes 4194304 | tf_op jit(solution)/shard_map/all_to_all | solution.py:474
  108.4 34.7 %collective-permute-start.18 = (bf16[512,1024]{1,0:T(8,128)(2,1)}, bf16[512,1024]{1,0:T(8,128)(2,1)S(1)}, u32[]{:S(2)}, u32[]{:S(2)}) collective-permute-start(bf16[512,1024]{1,0:T(8,128)(2,1)} %get-tuple-element.53), channel_id=1, source_target_pairs={{0,64},{16,80},{32,96},{48,112},{64,128},{80,144},{96,160},{112,17... | collective-permute-start | bytes 3145736 | tf_op jit(solution)/shard_map/ppermute | solution.py:493
  118.2 30.4 %collective-permute-start.19 = (bf16[512,1024]{1,0:T(8,128)(2,1)}, bf16[512,1024]{1,0:T(8,128)(2,1)}, u32[]{:S(2)}, u32[]{:S(2)}) collective-permute-start(bf16[512,1024]{1,0:T(8,128)(2,1)} %get-tuple-element.54), channel_id=1, source_target_pairs={{0,192},{16,208},{32,224},{48,240},{64,0},{80,16},{96,32},{112,48}... | collective-permute-start | bytes 3145736 | tf_op jit(solution)/shard_map/ppermute | solution.py:493
  119.6 46.9 %collective-permute-start.20 = (bf16[512,1024]{1,0:T(8,128)(2,1)}, bf16[512,1024]{1,0:T(8,128)(2,1)}, u32[]{:S(2)}, u32[]{:S(2)}) collective-permute-start(bf16[512,1024]{1,0:T(8,128)(2,1)} %get-tuple-element.55), channel_id=1, source_target_pairs={{0,128},{16,144},{32,160},{48,176},{64,192},{80,208},{96,224},{112... | collective-permute-start | bytes 3145736 | tf_op jit(solution)/shard_map/ppermute | solution.py:493
  125.5 56.7 %collective-permute-start.21 = (bf16[512,1024]{1,0:T(8,128)(2,1)}, bf16[512,1024]{1,0:T(8,128)(2,1)}, u32[]{:S(2)}, u32[]{:S(2)}) collective-permute-start(bf16[512,1024]{1,0:T(8,128)(2,1)} %get-tuple-element.60), channel_id=1, source_target_pairs={{0,16},{16,32},{32,48},{48,0},{64,80},{80,96},{96,112},{112,64},{1... | collective-permute-start | bytes 3145736 | tf_op jit(solution)/shard_map/ppermute | solution.py:493
  126.8 57.7 %collective-permute-start.22 = (bf16[512,1024]{1,0:T(8,128)(2,1)}, bf16[512,1024]{1,0:T(8,128)(2,1)}, u32[]{:S(2)}, u32[]{:S(2)}) collective-permute-start(bf16[512,1024]{1,0:T(8,128)(2,1)} %get-tuple-element.61), channel_id=1, source_target_pairs={{0,48},{16,0},{32,16},{48,32},{64,112},{80,64},{96,80},{112,96},{1... | collective-permute-start | bytes 3145736 | tf_op jit(solution)/shard_map/ppermute | solution.py:493
  144.1 40.4 %collective-permute-start.23 = (bf16[512,1024]{1,0:T(8,128)(2,1)}, bf16[512,1024]{1,0:T(8,128)(2,1)}, u32[]{:S(2)}, u32[]{:S(2)}) collective-permute-start(bf16[512,1024]{1,0:T(8,128)(2,1)} %get-tuple-element.62), channel_id=1, source_target_pairs={{0,32},{16,48},{32,0},{48,16},{64,96},{80,112},{96,64},{112,80},{1... | collective-permute-start | bytes 3145736 | tf_op jit(solution)/shard_map/ppermute | solution.py:493
  174.3 24.8 %all-to-all-start.1 = ((bf16[16,128,128]{2,1,0:T(8,128)(2,1)}), bf16[16,128,128]{2,1,0:T(8,128)(2,1)S(1)}, u32[]{:S(2)}, u32[]{:S(2)}) async-start(bf16[16,128,128]{2,1,0:T(8,128)(2,1)} %undo.1), calls=%async_computation.1 | async-start | bytes 1048576 | tf_op jit(solution)/shard_map/all_to_all | solution.py:513
  182.2 16.9 %collective-permute-start.26 = (bf16[128,1024]{1,0:T(8,128)(2,1)}, bf16[128,1024]{1,0:T(8,128)(2,1)S(1)}, u32[]{:S(2)}, u32[]{:S(2)}) collective-permute-start(bf16[128,1024]{1,0:T(8,128)(2,1)} %get-tuple-element.66), channel_id=1, source_target_pairs={{0,32},{16,48},{32,0},{48,16},{64,96},{80,112},{96,64},{112,80},{1... | collective-permute-start | bytes 786440 | tf_op jit(solution)/shard_map/ppermute | solution.py:500
  201.1 25.4 %all-to-all-start.2 = ((bf16[16,128,128]{2,1,0:T(8,128)(2,1)}), bf16[16,128,128]{2,1,0:T(8,128)(2,1)S(1)}, u32[]{:S(2)}, u32[]{:S(2)}) async-start(bf16[16,128,128]{2,1,0:T(8,128)(2,1)} %temporal.1), calls=%async_computation.2 | async-start | bytes 1048576 | tf_op jit(solution)/shard_map/all_to_all | solution.py:520
  209.6 16.2 %collective-permute-start.29 = (bf16[128,1024]{1,0:T(8,128)(2,1)}, bf16[128,1024]{1,0:T(8,128)(2,1)S(1)}, u32[]{:S(2)}, u32[]{:S(2)}) collective-permute-start(bf16[128,1024]{1,0:T(8,128)(2,1)} %get-tuple-element.69), channel_id=1, source_target_pairs={{0,128},{16,144},{32,160},{48,176},{64,192},{80,208},{96,224},{112... | collective-permute-start | bytes 786440 | tf_op jit(solution)/shard_map/ppermute | solution.py:500
  232.6 21.0 %all-to-all-start.3 = ((f32[16,32,128]{2,1,0:T(8,128)}), f32[16,32,128]{2,1,0:T(8,128)}, u32[]{:S(2)}, u32[]{:S(2)}) async-start(f32[16,32,128]{2,1,0:T(8,128)} %copy-done.37), calls=%async_computation.3 | async-start | bytes 524288 | tf_op jit(solution)/shard_map/all_to_all | solution.py:528
  (52 other events, 471.5 us)
where the time goes:
time: 265 us; the launch traced here: 259 us
  waiting for transfers between devices  109 us (41%)
  starting transfers between devices  84 us (32%)
  Pallas kernels  39 us (15%)
  local copies, waits for them, and re-layouts  21.2 us (8%)
  other arithmetic  4.35 us (2%)
    ppermute x6, waiting for transfers between devices, body(): lax.ppermute(parts[d], 'frame', axes[0][d])  32.8 us
    ppermute x6, waiting for transfers between devices, body(): moved = [lax.ppermute(parts[d], 'frame', axes[1][d]) for d in (1, 3, 2)]  23.7 us
    unnamed x84, local copies, waits for them, and re-layouts  21 us
    ppermute x2, waiting for transfers between devices, body(): lax.ppermute(x, 'expert', up)  18.5 us
    ppermute x6, starting transfers between devices, body(): lax.ppermute(parts[d], 'frame', axes[0][d])  18.3 us
    ppermute x2, waiting for transfers between devices, body(): chains.append([x, up1, lax.ppermute(up1, 'expert', up), down1])  17 us
    ppermute x2, waiting for transfers between devices, body(): up3 = lax.ppermute(packed[0], 'expert', up)  10.6 us
    all_to_all x1, starting transfers between devices, body(): lax.all_to_all(heads, 'expert', split_axis=0, concat_axis=0, tiled=True)  9.2 us
  transfers between devices with their start and end apart: 34, of which 13 were waited for; matrix products, arithmetic and copies ran while one was open for 2% of the time, Pallas kernels for 10%

commit v1 on v0

--- a/solution.py
+++ b/solution.py
@@ -35,6 +35,10 @@
 
 def iota(shape, dim):
     return lax.broadcasted_iota(jnp.int32, shape, dim)
+
+
+def pinned(*arrays):
+    return [pltpu.with_memory_space_constraint(a, pltpu.HBM) for a in arrays]
 
 
 def call(kernel, out_shape, name, **kw):
@@ -251,7 +255,7 @@
     return row, e1, e2, e4, s4, shifted
 
 
-def undo_kernel(undo, returned, after, mixed):
+def undo_kernel(undo, returned, mixed):
     blocks = mixed.shape[0]
     pick = undo[...]
     step = 512
@@ -345,12 +349,11 @@
     scratch[...] = carry
     back = (order_row[...] == iota((rows, rows), 0)).astype(jnp.float32).astype(jnp.bfloat16)
     first = pl.program_id(0) * (width // LANES)
-    for b in range(width // LANES):
-        at = slice(b * LANES, (b + 1) * LANES)
-        value = base[:, at] + reach[:, at] * scratch[pl.ds(first + b, 1), :]
-        out[:, at] = jnp.dot(
-            back, value.astype(jnp.bfloat16), preferred_element_type=jnp.float32
-        ).astype(jnp.bfloat16)
+    spread = [scratch[pl.ds(first + b, 1), :] for b in range(width // LANES)]
+    value = base[...] + reach[...] * jnp.concatenate(spread, axis=1)
+    out[...] = jnp.dot(
+        back, value.astype(jnp.bfloat16), preferred_element_type=jnp.float32
+    ).astype(jnp.bfloat16)
 
 
 def body(
@@ -395,7 +398,7 @@
         in_specs=[far, vmem, vmem],
         out_specs=far,
         scratch_shapes=[pltpu.VMEM((rows, LANES), bf16), pltpu.SemaphoreType.DMA((2,))],
-    )(saved[0], ids_col.T, gates[0].T)
+    )(*pinned(saved[0]), ids_col.T, gates[0].T)
     chains = []
     for x in (marked, upstream[0]):
         up1, down1 = lax.ppermute(x, "expert", up), lax.ppermute(x, "expert", down)
@@ -447,7 +450,7 @@
         forward_kernel,
         (
             pltpu.HBM((slots, width), bf16),
-            shape((slots, hidden_width), bf16),
+            pltpu.HBM((slots, hidden_width), bf16),
             shape((slots, hidden_width), f32),
         ),
         "forward",
@@ -478,7 +481,7 @@
     place = jnp.stack([frame // 4, frame % 4]).astype(jnp.int32)
     along_x = [[(i, (i // 4 + d) % 4 * 4 + i % 4) for i in range(frames)] for d in range(4)]
     along_y = [[(i, i // 4 * 4 + (i % 4 + d) % 4) for i in range(frames)] for d in range(4)]
-    grads, sums, moves = [], [], []
+    grads, sums = [], []
     for name, left, right, axes, turn in (
         ("grads_out", routed_all, hidden, (along_x, along_y), 1),
         ("grads_in", inputs_all, back_pre, (along_y, along_x), 0),
@@ -489,17 +492,16 @@
             (pltpu.HBM(quarter, bf16),) * 4,
             name,
             in_specs=[smem] + [vmem] * 2,
-        )(place, left, right)
+        )(place, *pinned(left, right))
         parts = [parts[0]] + [lax.ppermute(parts[d], "frame", axes[0][d]) for d in (1, 3, 2)]
         parts = call(
             functools.partial(sum_kernel, turn),
             tuple(pltpu.HBM((LANES, hidden_width), bf16 if d else f32) for d in range(4)),
             "sum_" + name,
             in_specs=[smem] + [vmem] * 4,
-        )(place, *parts)
+        )(place, *pinned(parts[0]), *parts[1:])
         moved = [lax.ppermute(parts[d], "frame", axes[1][d]) for d in (1, 3, 2)]
-        sums.append(parts[0])
-        moves.append(moved)
+        sums += pinned(parts[0])
         total = parts[0] + moved[0].astype(f32) + moved[1].astype(f32) + moved[2].astype(f32)
         grads.append(total.astype(bf16)[None])
     grad_out, grad_in = grads
@@ -508,23 +510,22 @@
         undo_kernel,
         shape((blocks, rows, LANES), bf16),
         "undo",
-        in_specs=[vmem, vmem, far],
-    )(undo, returned, sums[0])
+    )(undo, returned)
     pencil = lax.all_to_all(mixed, "frame", split_axis=0, concat_axis=0, tiled=True)
     pencil = call(
         temporal_kernel,
         shape(pencil.shape, bf16),
         "temporal",
-        in_specs=[vmem] * 3 + [far] * 4,
-    )(pencil, keep_time, inject_time, sums[1], *moves[0])
+        in_specs=[vmem] * 3 + [far],
+    )(pencil, keep_time, inject_time, sums[0])
     spatial = lax.all_to_all(pencil, "frame", split_axis=0, concat_axis=0, tiled=True)
     local, heads = call(
         scan_kernel,
-        (shape((rows, width), f32), shape((experts, 2 * blocks, LANES), f32)),
+        (pltpu.HBM((rows, width), f32), pltpu.HBM((experts, 2 * blocks, LANES), f32)),
         "scan",
-        in_specs=[vmem] * 2 + [far] * 3,
+        in_specs=[vmem] * 2 + [far],
         scratch_shapes=[pltpu.VMEM((2 * blocks, LANES), f32)],
-    )(spatial, rate, *moves[1])
+    )(spatial, rate, sums[1])
     heads = lax.all_to_all(heads, "expert", split_axis=0, concat_axis=0, tiled=True)
     base, reach = call(combine_kernel, (pltpu.HBM((rows, width), f32),) * 2, "combine")(
         rate, inject, local, ordered
@@ -544,7 +545,7 @@
         ],
         out_specs=chunk,
         scratch_shapes=[pltpu.VMEM((blocks, LANES), f32)],
-    )(scalar, local_order.reshape(1, rows), heads, base, reach)
+    )(scalar, local_order.reshape(1, rows), heads, *pinned(base, reach))
     return (result[None], grad_in, grad_out)
 
 

time: 265 us -> 249 us (0.940)
  Pallas kernels: 39 us -> 60.6 us
  waiting for transfers between devices: 109 us -> 88.3 us
  local copies, waits for them, and re-layouts: 21.2 us -> 3.45 us
    unnamed x84 -> x32, local copies, waits for them, and re-layouts: 21 us -> 3.18 us
    ppermute x6, waiting for transfers between devices: 23.7 us -> 6.57 us  [body(): moved = [lax.ppermute(parts[d], 'frame', axes[1][d]) for d in (1, 3, 2)]]
    pallas_call x1, Pallas kernels: 0.85 us -> 17 us  [body(): call(facts_kernel, pltpu.HBM((rows, width + LANES), bf16), 'facts', in_sp...]
    ppermute x6, waiting for transfers between devices: 32.8 us -> 19.8 us  [body(): lax.ppermute(parts[d], 'frame', axes[0][d])]
    all_to_all x1, waiting for transfers between devices: 0.01 us -> 12.4 us  [body(): lax.all_to_all(mixed, 'frame', split_axis=0, concat_axis=0, tiled=True)]
    all_to_all x1, waiting for transfers between devices: 6.84 us -> 0.01 us  [body(): lax.all_to_all(heads, 'expert', split_axis=0, concat_axis=0, tiled=True)]
    all_to_all x1, waiting for transfers between devices: 0.01 us -> 3.46 us  [body(): lax.all_to_all(back_slots, 'expert', split_axis=0, concat_axis=0, tiled=T...]
  transfers between devices with their start and end apart: 34 -> 34, of which waited for: 13 -> 11; matrix products, arithmetic and copies ran while one was open for 2% -> 2% of each run, Pallas kernels for 10% -> 14%
where the time goes in v1:
time: 249 us; the launch traced here: 244 us
  waiting for transfers between devices  88.3 us (35%)
  starting transfers between devices  84.9 us (34%)
  Pallas kernels  60.6 us (24%)
  other arithmetic  5.6 us (2%)
  local copies, waits for them, and re-layouts  3.45 us (1%)
    ppermute x6, waiting for transfers between devices, body(): lax.ppermute(parts[d], 'frame', axes[0][d])  19.8 us
    ppermute x2, waiting for transfers between devices, body(): lax.ppermute(x, 'expert', up)  18.5 us
    ppermute x6, starting transfers between devices, body(): lax.ppermute(parts[d], 'frame', axes[0][d])  18.3 us
    pallas_call x1, Pallas kernels, body(): call(facts_kernel, pltpu.HBM((rows, width + LANES), bf16), 'facts', in_sp...  17 us
    ppermute x2, waiting for transfers between devices, body(): chains.append([x, up1, lax.ppermute(up1, 'expert', up), down1])  17 us
    all_to_all x1, waiting for transfers between devices, body(): lax.all_to_all(mixed, 'frame', split_axis=0, concat_axis=0, tiled=True)  12.4 us
    ppermute x2, waiting for transfers between devices, body(): up3 = lax.ppermute(packed[0], 'expert', up)  10.6 us
    pallas_call x2, Pallas kernels, body(): call(functools.partial(grads_kernel, scale, turn == 0), (pltpu.HBM(quarte...  10.5 us
  transfers between devices with their start and end apart: 34, of which 11 were waited for; matrix products, arithmetic and copies ran while one was open for 2% of the time, Pallas kernels for 14%

profile of v1, /device:TPU:1, one launch (start us, length us, event | category | flops | bytes accessed | tf_op | source)
XLA Modules:
  0.0 244.0 jit_solution(9983719817931981268)
XLA Ops:
  2.0 17.0 %facts.1.refs_0_.refs_5_ = bf16[128,2176]{1,0:T(8,128)(2,1)} custom-call(bf16[128,2048]{1,0:T(8,128)(2,1)} %bitcast.38, s32[2,128]{1,0:T(2,128)S(1)} %bitcast.35, f32[2,128]{1,0:T(2,128)S(1)} %bitcast.37), custom_call_target="tpu_custom_call" | custom-call | tf_op jit(solution)/shard_map/facts/pallas_call | solution.py:394
  21.5 4.0 %collective-permute-start.2 = (bf16[128,2176]{1,0:T(8,128)(2,1)}, bf16[128,2176]{1,0:T(8,128)(2,1)S(1)}, u32[]{:S(2)}, u32[]{:S(2)}) collective-permute-start(bf16[128,2176]{1,0:T(8,128)(2,1)} %facts.1.refs_0_.refs_5_), channel_id=1, source_target_pairs={{0,14},{1,15},{2,0},{3,1},{4,2},{5,3},{6,4},{7,5},{8,6},{9,7},{10,... | collective-permute-start | bytes 1671176 | tf_op jit(solution)/shard_map/ppermute | solution.py:404
  28.2 9.8 %collective-permute-done.refs_1_.refs_6_ = bf16[128,2176]{1,0:T(8,128)(2,1)S(1)} collective-permute-done((bf16[128,2176]{1,0:T(8,128)(2,1)}, bf16[128,2176]{1,0:T(8,128)(2,1)S(1)}, u32[]{:S(2)}, u32[]{:S(2)}) %collective-permute-start) | collective-permute-done | bytes 557088 | tf_op jit(solution)/shard_map/ppermute | solution.py:404
  40.7 8.7 %collective-permute-done.4.refs_6_ = bf16[128,2048]{1,0:T(8,128)(2,1)} collective-permute-done((bf16[128,2048]{1,0:T(8,128)(2,1)}, bf16[128,2048]{1,0:T(8,128)(2,1)}, u32[]{:S(2)}, u32[]{:S(2)}) %collective-permute-start.4) | collective-permute-done | bytes 524320 | tf_op jit(solution)/shard_map/ppermute | solution.py:404
  52.1 9.2 %collective-permute-done.1.facts_up.refs_2_.up.refs_7_ = bf16[128,2176]{1,0:T(8,128)(2,1)S(1)} collective-permute-done((bf16[128,2176]{1,0:T(8,128)(2,1)S(1)}, bf16[128,2176]{1,0:T(8,128)(2,1)S(1)}, u32[]{:S(2)}, u32[]{:S(2)}) %collective-permute-start.1) | collective-permute-done | bytes 557088 | tf_op jit(solution)/shard_map/ppermute | solution.py:405
  64.6 7.8 %collective-permute-done.5.up.refs_7_ = bf16[128,2048]{1,0:T(8,128)(2,1)S(1)} collective-permute-done((bf16[128,2048]{1,0:T(8,128)(2,1)}, bf16[128,2048]{1,0:T(8,128)(2,1)S(1)}, u32[]{:S(2)}, u32[]{:S(2)}) %collective-permute-start.5) | collective-permute-done | bytes 524320 | tf_op jit(solution)/shard_map/ppermute | solution.py:405
  75.9 5.0 %collective-permute-done.13.refs_10_ = bf16[96,2048]{1,0:T(8,128)(2,1)S(1)} collective-permute-done((bf16[96,2048]{1,0:T(8,128)(2,1)S(1)}, bf16[96,2048]{1,0:T(8,128)(2,1)S(1)}, u32[]{:S(2)}, u32[]{:S(2)}) %collective-permute-start.13) | collective-permute-done | bytes 393248 | tf_op jit(solution)/shard_map/ppermute | solution.py:419
  83.7 5.6 %collective-permute-done.8.refs_10_ = bf16[96,2048]{1,0:T(8,128)(2,1)S(1)} collective-permute-done((bf16[96,2048]{1,0:T(8,128)(2,1)S(1)}, bf16[96,2048]{1,0:T(8,128)(2,1)S(1)}, u32[]{:S(2)}, u32[]{:S(2)}) %collective-permute-start.8) | collective-permute-done | bytes 393248 | tf_op jit(solution)/shard_map/ppermute | solution.py:419
  100.4 4.5 %forward.1 = (bf16[512,2048]{1,0:T(8,128)(2,1)}, bf16[512,1024]{1,0:T(8,128)(2,1)}, f32[512,1024]{1,0:T(8,128)S(1)}) custom-call(bf16[256,2048]{1,0:T(8,128)(2,1)S(1)} %get-tuple-element.46.own, bf16[256,2048]{1,0:T(8,128)(2,1)S(1)} %collective-permute-done.17.got, bf16[2048,1024]{1,0:T(8,128)(2,1)S(1)} %bitcast.25), custom_call_target="tpu_custom_call" | custom-call | tf_op jit(solution)/shard_map/forward/pallas_call | solution.py:449
  104.9 5.6 %backward.1 = (bf16[512,2048]{1,0:T(8,128)(2,1)}, bf16[512,1024]{1,0:T(8,128)(2,1)}, bf16[16,32,2048]{2,1,0:T(8,128)(2,1)}) custom-call(s32[1]{0:T(128)} %bitcast.me, bf16[256,2048]{1,0:T(8,128)(2,1)S(1)} %get-tuple-element.42.own, bf16[256,2048]{1,0:T(8,128)(2,1)S(1)} %collective-permute-done.12.got, bf16[2048,1024]{1,0:T(8,128)(2,1)S(1)} %bitcast.30, ...), custom_call_target="tpu_custom_call" | custom-call | tf_op jit(solution)/shard_map/backward/pallas_call | solution.py:460
  110.5 6.7 %all-to-all-start = ((bf16[16,32,2048]{2,1,0:T(8,128)(2,1)}), bf16[16,32,2048]{2,1,0:T(8,128)(2,1)S(1)}, u32[]{:S(2)}, u32[]{:S(2)}) async-start(bf16[16,32,2048]{2,1,0:T(8,128)(2,1)} %get-tuple-element.49), calls=%async_computation | async-start | bytes 4194304 | tf_op jit(solution)/shard_map/all_to_all | solution.py:477
  117.3 5.2 %grads_out.1 = (bf16[512,1024]{1,0:T(8,128)(2,1)}, bf16[512,1024]{1,0:T(8,128)(2,1)}, bf16[512,1024]{1,0:T(8,128)(2,1)}, bf16[512,1024]{1,0:T(8,128)(2,1)}) custom-call(s32[2]{0:T(128)S(1)} %pad_add_fusion.place, bf16[512,2048]{1,0:T(8,128)(2,1)} %get-tuple-element.50.left, bf16[512,1024]{1,0:T(8,128)(2,1)} %get-tuple-element.51.right), custom_call_target="tpu_custom_call" | custom-call | tf_op jit(solution)/shard_map/grads_out/pallas_call | solution.py:490
  122.5 9.8 %collective-permute-start.18 = (bf16[512,1024]{1,0:T(8,128)(2,1)}, bf16[512,1024]{1,0:T(8,128)(2,1)S(1)}, u32[]{:S(2)}, u32[]{:S(2)}) collective-permute-start(bf16[512,1024]{1,0:T(8,128)(2,1)} %get-tuple-element.53), channel_id=1, source_target_pairs={{0,64},{16,80},{32,96},{48,112},{64,128},{80,144},{96,160},{112,17... | collective-permute-start | bytes 3145736 | tf_op jit(solution)/shard_map/ppermute | solution.py:496
  135.3 5.3 %grads_in.1 = (bf16[512,1024]{1,0:T(8,128)(2,1)}, bf16[512,1024]{1,0:T(8,128)(2,1)}, bf16[512,1024]{1,0:T(8,128)(2,1)}, bf16[512,1024]{1,0:T(8,128)(2,1)}) custom-call(s32[2]{0:T(128)S(1)} %pad_add_fusion.place, bf16[512,2048]{1,0:T(8,128)(2,1)} %get-tuple-element.57.left, bf16[512,1024]{1,0:T(8,128)(2,1)} %get-tuple-element.58.right), custom_call_target="tpu_custom_call" | custom-call | tf_op jit(solution)/shard_map/grads_in/pallas_call | solution.py:490
  143.3 13.9 %collective-permute-done.18.p1 = bf16[512,1024]{1,0:T(8,128)(2,1)S(1)} collective-permute-done((bf16[512,1024]{1,0:T(8,128)(2,1)}, bf16[512,1024]{1,0:T(8,128)(2,1)S(1)}, u32[]{:S(2)}, u32[]{:S(2)}) %collective-permute-start.18) | collective-permute-done | bytes 1048608 | tf_op jit(solution)/shard_map/ppermute | solution.py:496
  162.7 3.5 %all-to-all-done = bf16[16,32,2048]{2,1,0:T(8,128)(2,1)S(1)} async-done(((bf16[16,32,2048]{2,1,0:T(8,128)(2,1)}), bf16[16,32,2048]{2,1,0:T(8,128)(2,1)S(1)}, u32[]{:S(2)}, u32[]{:S(2)}) %all-to-all-start) | async-done | bytes 2097184 | tf_op jit(solution)/shard_map/all_to_all | solution.py:477
  167.4 6.8 %all-to-all-start.1 = ((bf16[16,128,128]{2,1,0:T(8,128)(2,1)}), bf16[16,128,128]{2,1,0:T(8,128)(2,1)S(1)}, u32[]{:S(2)}, u32[]{:S(2)}) async-start(bf16[16,128,128]{2,1,0:T(8,128)(2,1)} %undo.1), calls=%async_computation.1 | async-start | bytes 1048576 | tf_op jit(solution)/shard_map/all_to_all | solution.py:514
  174.9 5.8 %collective-permute-done.20.p3 = bf16[512,1024]{1,0:T(8,128)(2,1)} collective-permute-done((bf16[512,1024]{1,0:T(8,128)(2,1)}, bf16[512,1024]{1,0:T(8,128)(2,1)}, u32[]{:S(2)}, u32[]{:S(2)}) %collective-permute-start.20) | collective-permute-done | bytes 1048608 | tf_op jit(solution)/shard_map/ppermute | solution.py:496
  184.0 12.4 %all-to-all-done.1.pencil = bf16[16,128,128]{2,1,0:T(8,128)(2,1)S(1)} async-done(((bf16[16,128,128]{2,1,0:T(8,128)(2,1)}), bf16[16,128,128]{2,1,0:T(8,128)(2,1)S(1)}, u32[]{:S(2)}, u32[]{:S(2)}) %all-to-all-start.1) | async-done | bytes 524320 | tf_op jit(solution)/shard_map/all_to_all | solution.py:514
  197.3 4.0 %all-to-all-start.2 = ((bf16[16,128,128]{2,1,0:T(8,128)(2,1)}), bf16[16,128,128]{2,1,0:T(8,128)(2,1)S(1)}, u32[]{:S(2)}, u32[]{:S(2)}) async-start(bf16[16,128,128]{2,1,0:T(8,128)(2,1)} %temporal.1), calls=%async_computation.2 | async-start | bytes 1048576 | tf_op jit(solution)/shard_map/all_to_all | solution.py:521
  201.4 3.7 %sum_grads_in.1 = (f32[128,1024]{1,0:T(8,128)}, bf16[128,1024]{1,0:T(8,128)(2,1)}, bf16[128,1024]{1,0:T(8,128)(2,1)}, bf16[128,1024]{1,0:T(8,128)(2,1)}) custom-call(s32[2]{0:T(128)S(1)} %pad_add_fusion.place, bf16[512,1024]{1,0:T(8,128)(2,1)} %get-tuple-element.59.p0, bf16[512,1024]{1,0:T(8,128)(2,1)} %collective-permute-done.21.p1, ...), custom_call_target="tpu_custom_call" | custom-call | tf_op jit(solution)/shard_map/sum_grads_in/pallas_call | solution.py:497
  216.4 10.0 %all-to-all-start.3 = ((f32[16,32,128]{2,1,0:T(8,128)}), f32[16,32,128]{2,1,0:T(8,128)S(1)}, u32[]{:S(2)}, u32[]{:S(2)}) async-start(f32[16,32,128]{2,1,0:T(8,128)} %get-tuple-element.64), calls=%async_computation.3 | async-start | bytes 524288 | tf_op jit(solution)/shard_map/all_to_all | solution.py:529
  229.2 6.6 %collective-permute-done.27 = bf16[128,1024]{1,0:T(8,128)(2,1)S(1)} collective-permute-done((bf16[128,1024]{1,0:T(8,128)(2,1)}, bf16[128,1024]{1,0:T(8,128)(2,1)S(1)}, u32[]{:S(2)}, u32[]{:S(2)}) %collective-permute-start.27) | collective-permute-done | bytes 262176 | tf_op jit(solution)/shard_map/ppermute | solution.py:503
  239.9 3.9 %finish.1 = bf16[128,2048]{1,0:T(8,128)(2,1)} custom-call(s32[1]{0:T(128)} %bitcast.me, s32[1,128]{1,0:T(1,128)S(1)} %get-tuple-element.78.order_row, f32[16,32,128]{2,1,0:T(8,128)S(1)} %all-to-all-done.3.heads, f32[128,2048]{1,0:T(8,128)} %get-tuple-element.67.base, f32[128,2048]{1,0:T(8,128)} %get-tuple-element.68.reach), custom_call_target="tpu_custom_call" | custom-call | tf_op jit(solution)/shard_map/finish/pallas_call | solution.py:534
  (105 shorter events, 68.2 us)
Async XLA Ops:
  19.0 19.0 %collective-permute-start = (bf16[128,2176]{1,0:T(8,128)(2,1)}, bf16[128,2176]{1,0:T(8,128)(2,1)S(1)}, u32[]{:S(2)}, u32[]{:S(2)}) collective-permute-start(bf16[128,2176]{1,0:T(8,128)(2,1)} %facts.1.refs_0_.refs_5_), channel_id=1, source_target_pairs={{0,2},{1,3},{2,4},{3,5},{4,6},{5,7},{6,8},{7,9},{8,10},{9,11},{10,... | collective-permute-start | bytes 1671176 | tf_op jit(solution)/shard_map/ppermute | solution.py:404
  21.5 16.5 %collective-permute-start.2 = (bf16[128,2176]{1,0:T(8,128)(2,1)}, bf16[128,2176]{1,0:T(8,128)(2,1)S(1)}, u32[]{:S(2)}, u32[]{:S(2)}) collective-permute-start(bf16[128,2176]{1,0:T(8,128)(2,1)} %facts.1.refs_0_.refs_5_), channel_id=1, source_target_pairs={{0,14},{1,15},{2,0},{3,1},{4,2},{5,3},{6,4},{7,5},{8,6},{9,7},{10,... | collective-permute-start | bytes 1671176 | tf_op jit(solution)/shard_map/ppermute | solution.py:404
  25.6 23.8 %collective-permute-start.4 = (bf16[128,2048]{1,0:T(8,128)(2,1)}, bf16[128,2048]{1,0:T(8,128)(2,1)}, u32[]{:S(2)}, u32[]{:S(2)}) collective-permute-start(bf16[128,2048]{1,0:T(8,128)(2,1)} %bitcast.31), channel_id=1, source_target_pairs={{0,2},{1,3},{2,4},{3,5},{4,6},{5,7},{6,8},{7,9},{8,10},{9,11},{10,... | collective-permute-start | bytes 1572872 | tf_op jit(solution)/shard_map/ppermute | solution.py:404
  25.6 23.8 %collective-permute-start.6 = (bf16[128,2048]{1,0:T(8,128)(2,1)}, bf16[128,2048]{1,0:T(8,128)(2,1)}, u32[]{:S(2)}, u32[]{:S(2)}) collective-permute-start(bf16[128,2048]{1,0:T(8,128)(2,1)} %bitcast.32), channel_id=1, source_target_pairs={{0,14},{1,15},{2,0},{3,1},{4,2},{5,3},{6,4},{7,5},{8,6},{9,7},{10,... | collective-permute-start | bytes 1572872 | tf_op jit(solution)/shard_map/ppermute | solution.py:404
  38.0 23.2 %collective-permute-start.1 = (bf16[128,2176]{1,0:T(8,128)(2,1)S(1)}, bf16[128,2176]{1,0:T(8,128)(2,1)S(1)}, u32[]{:S(2)}, u32[]{:S(2)}) collective-permute-start(bf16[128,2176]{1,0:T(8,128)(2,1)S(1)} %collective-permute-done.refs_1_.refs_6_), channel_id=1, source_target_pairs={{0,2},{1,3},{2,4},{3,5},{4,6},{5,7},{6,8},{7,9},{8,10},{9,11},{10,... | collective-permute-start | bytes 1671176 | tf_op jit(solution)/shard_map/ppermute | solution.py:405
  38.1 23.2 %collective-permute-start.3 = (bf16[128,2176]{1,0:T(8,128)(2,1)S(1)}, bf16[128,2176]{1,0:T(8,128)(2,1)S(1)}, u32[]{:S(2)}, u32[]{:S(2)}) collective-permute-start(bf16[128,2176]{1,0:T(8,128)(2,1)S(1)} %collective-permute-done.2.refs_3_.refs_8_), channel_id=1, source_target_pairs={{0,14},{1,15},{2,0},{3,1},{4,2},{5,3},{6,4},{7,5},{8,6},{9,7},{10,... | collective-permute-start | bytes 1671176 | tf_op jit(solution)/shard_map/ppermute | solution.py:406
  49.4 23.1 %collective-permute-start.5 = (bf16[128,2048]{1,0:T(8,128)(2,1)}, bf16[128,2048]{1,0:T(8,128)(2,1)S(1)}, u32[]{:S(2)}, u32[]{:S(2)}) collective-permute-start(bf16[128,2048]{1,0:T(8,128)(2,1)} %collective-permute-done.4.refs_6_), channel_id=1, source_target_pairs={{0,2},{1,3},{2,4},{3,5},{4,6},{5,7},{6,8},{7,9},{8,10},{9,11},{10,... | collective-permute-start | bytes 1572872 | tf_op jit(solution)/shard_map/ppermute | solution.py:405
  49.4 23.1 %collective-permute-start.7 = (bf16[128,2048]{1,0:T(8,128)(2,1)}, bf16[128,2048]{1,0:T(8,128)(2,1)S(1)}, u32[]{:S(2)}, u32[]{:S(2)}) collective-permute-start(bf16[128,2048]{1,0:T(8,128)(2,1)} %collective-permute-done.6.refs_8_), channel_id=1, source_target_pairs={{0,14},{1,15},{2,0},{3,1},{4,2},{5,3},{6,4},{7,5},{8,6},{9,7},{10,... | collective-permute-start | bytes 1572872 | tf_op jit(solution)/shard_map/ppermute | solution.py:406
  61.9 19.0 %collective-permute-start.13 = (bf16[96,2048]{1,0:T(8,128)(2,1)S(1)}, bf16[96,2048]{1,0:T(8,128)(2,1)S(1)}, u32[]{:S(2)}, u32[]{:S(2)}) collective-permute-start(bf16[96,2048]{1,0:T(8,128)(2,1)S(1)} %get-tuple-element.44), channel_id=1, source_target_pairs={{0,2},{1,3},{2,4},{3,5},{4,6},{5,7},{6,8},{7,9},{8,10},{9,11},{10,... | collective-permute-start | bytes 1179656 | tf_op jit(solution)/shard_map/ppermute | solution.py:419
  61.9 19.0 %collective-permute-start.14 = (bf16[96,2048]{1,0:T(8,128)(2,1)S(1)}, bf16[96,2048]{1,0:T(8,128)(2,1)S(1)}, u32[]{:S(2)}, u32[]{:S(2)}) collective-permute-start(bf16[96,2048]{1,0:T(8,128)(2,1)S(1)} %get-tuple-element.45), channel_id=1, source_target_pairs={{0,14},{1,15},{2,0},{3,1},{4,2},{5,3},{6,4},{7,5},{8,6},{9,7},{10,... | collective-permute-start | bytes 1179656 | tf_op jit(solution)/shard_map/ppermute | solution.py:420
  110.5 55.6 %all-to-all-start = ((bf16[16,32,2048]{2,1,0:T(8,128)(2,1)}), bf16[16,32,2048]{2,1,0:T(8,128)(2,1)S(1)}, u32[]{:S(2)}, u32[]{:S(2)}) async-start(bf16[16,32,2048]{2,1,0:T(8,128)(2,1)} %get-tuple-element.49), calls=%async_computation | async-start | bytes 4194304 | tf_op jit(solution)/shard_map/all_to_all | solution.py:477
  122.5 34.7 %collective-permute-start.18 = (bf16[512,1024]{1,0:T(8,128)(2,1)}, bf16[512,1024]{1,0:T(8,128)(2,1)S(1)}, u32[]{:S(2)}, u32[]{:S(2)}) collective-permute-start(bf16[512,1024]{1,0:T(8,128)(2,1)} %get-tuple-element.53), channel_id=1, source_target_pairs={{0,64},{16,80},{32,96},{48,112},{64,128},{80,144},{96,160},{112,17... | collective-permute-start | bytes 3145736 | tf_op jit(solution)/shard_map/ppermute | solution.py:496
  132.3 42.6 %collective-permute-start.19 = (bf16[512,1024]{1,0:T(8,128)(2,1)}, bf16[512,1024]{1,0:T(8,128)(2,1)}, u32[]{:S(2)}, u32[]{:S(2)}) collective-permute-start(bf16[512,1024]{1,0:T(8,128)(2,1)} %get-tuple-element.54), channel_id=1, source_target_pairs={{0,192},{16,208},{32,224},{48,240},{64,0},{80,16},{96,32},{112,48}... | collective-permute-start | bytes 3145736 | tf_op jit(solution)/shard_map/ppermute | solution.py:496
  133.7 47.0 %collective-permute-start.20 = (bf16[512,1024]{1,0:T(8,128)(2,1)}, bf16[512,1024]{1,0:T(8,128)(2,1)}, u32[]{:S(2)}, u32[]{:S(2)}) collective-permute-start(bf16[512,1024]{1,0:T(8,128)(2,1)} %get-tuple-element.55), channel_id=1, source_target_pairs={{0,128},{16,144},{32,160},{48,176},{64,192},{80,208},{96,224},{112... | collective-permute-start | bytes 3145736 | tf_op jit(solution)/shard_map/ppermute | solution.py:496
  140.5 60.8 %collective-permute-start.21 = (bf16[512,1024]{1,0:T(8,128)(2,1)}, bf16[512,1024]{1,0:T(8,128)(2,1)}, u32[]{:S(2)}, u32[]{:S(2)}) collective-permute-start(bf16[512,1024]{1,0:T(8,128)(2,1)} %get-tuple-element.60), channel_id=1, source_target_pairs={{0,16},{16,32},{32,48},{48,0},{64,80},{80,96},{96,112},{112,64},{1... | collective-permute-start | bytes 3145736 | tf_op jit(solution)/shard_map/ppermute | solution.py:496
  141.8 59.5 %collective-permute-start.22 = (bf16[512,1024]{1,0:T(8,128)(2,1)}, bf16[512,1024]{1,0:T(8,128)(2,1)}, u32[]{:S(2)}, u32[]{:S(2)}) collective-permute-start(bf16[512,1024]{1,0:T(8,128)(2,1)} %get-tuple-element.61), channel_id=1, source_target_pairs={{0,48},{16,0},{32,16},{48,32},{64,112},{80,64},{96,80},{112,96},{1... | collective-permute-start | bytes 3145736 | tf_op jit(solution)/shard_map/ppermute | solution.py:496
  158.2 43.2 %collective-permute-start.23 = (bf16[512,1024]{1,0:T(8,128)(2,1)}, bf16[512,1024]{1,0:T(8,128)(2,1)}, u32[]{:S(2)}, u32[]{:S(2)}) collective-permute-start(bf16[512,1024]{1,0:T(8,128)(2,1)} %get-tuple-element.62), channel_id=1, source_target_pairs={{0,32},{16,48},{32,0},{48,16},{64,96},{80,112},{96,64},{112,80},{1... | collective-permute-start | bytes 3145736 | tf_op jit(solution)/shard_map/ppermute | solution.py:496
  167.4 29.0 %all-to-all-start.1 = ((bf16[16,128,128]{2,1,0:T(8,128)(2,1)}), bf16[16,128,128]{2,1,0:T(8,128)(2,1)S(1)}, u32[]{:S(2)}, u32[]{:S(2)}) async-start(bf16[16,128,128]{2,1,0:T(8,128)(2,1)} %undo.1), calls=%async_computation.1 | async-start | bytes 1048576 | tf_op jit(solution)/shard_map/all_to_all | solution.py:514
  197.3 16.6 %all-to-all-start.2 = ((bf16[16,128,128]{2,1,0:T(8,128)(2,1)}), bf16[16,128,128]{2,1,0:T(8,128)(2,1)S(1)}, u32[]{:S(2)}, u32[]{:S(2)}) async-start(bf16[16,128,128]{2,1,0:T(8,128)(2,1)} %temporal.1), calls=%async_computation.2 | async-start | bytes 1048576 | tf_op jit(solution)/shard_map/all_to_all | solution.py:521
  205.1 21.4 %collective-permute-start.26 = (bf16[128,1024]{1,0:T(8,128)(2,1)}, bf16[128,1024]{1,0:T(8,128)(2,1)}, u32[]{:S(2)}, u32[]{:S(2)}) collective-permute-start(bf16[128,1024]{1,0:T(8,128)(2,1)} %get-tuple-element.71), channel_id=1, source_target_pairs={{0,128},{16,144},{32,160},{48,176},{64,192},{80,208},{96,224},{112... | collective-permute-start | bytes 786440 | tf_op jit(solution)/shard_map/ppermute | solution.py:503
  207.9 19.2 %collective-permute-start.25 = (bf16[128,1024]{1,0:T(8,128)(2,1)}, bf16[128,1024]{1,0:T(8,128)(2,1)}, u32[]{:S(2)}, u32[]{:S(2)}) collective-permute-start(bf16[128,1024]{1,0:T(8,128)(2,1)} %get-tuple-element.70), channel_id=1, source_target_pairs={{0,192},{16,208},{32,224},{48,240},{64,0},{80,16},{96,32},{112,48}... | collective-permute-start | bytes 786440 | tf_op jit(solution)/shard_map/ppermute | solution.py:503
  208.8 18.3 %collective-permute-start.24 = (bf16[128,1024]{1,0:T(8,128)(2,1)}, bf16[128,1024]{1,0:T(8,128)(2,1)}, u32[]{:S(2)}, u32[]{:S(2)}) collective-permute-start(bf16[128,1024]{1,0:T(8,128)(2,1)} %get-tuple-element.69), channel_id=1, source_target_pairs={{0,64},{16,80},{32,96},{48,112},{64,128},{80,144},{96,160},{112,17... | collective-permute-start | bytes 786440 | tf_op jit(solution)/shard_map/ppermute | solution.py:503
  210.0 19.2 %collective-permute-start.29 = (bf16[128,1024]{1,0:T(8,128)(2,1)}, bf16[128,1024]{1,0:T(8,128)(2,1)}, u32[]{:S(2)}, u32[]{:S(2)}) collective-permute-start(bf16[128,1024]{1,0:T(8,128)(2,1)} %get-tuple-element.74), channel_id=1, source_target_pairs={{0,32},{16,48},{32,0},{48,16},{64,96},{80,112},{96,64},{112,80},{1... | collective-permute-start | bytes 786440 | tf_op jit(solution)/shard_map/ppermute | solution.py:503
  216.4 23.5 %all-to-all-start.3 = ((f32[16,32,128]{2,1,0:T(8,128)}), f32[16,32,128]{2,1,0:T(8,128)S(1)}, u32[]{:S(2)}, u32[]{:S(2)}) async-start(f32[16,32,128]{2,1,0:T(8,128)} %get-tuple-element.64), calls=%async_computation.3 | async-start | bytes 524288 | tf_op jit(solution)/shard_map/all_to_all | solution.py:529
  (26 other events, 329.7 us)
